TPU v7x, 32 devices: a whole 2x2x4 slice. The times are simulated.
32 devices in a mesh: seq: 4 (over y, x), tensor: 8 (over z, core).
Axes of the slice: x: 2, y: 2, z: 4, core: 2. Of those that a mesh axis runs over, the one named last changes fastest.
Arguments:
- tokens: bfloat16 [1024, 4096], P(('seq', 'tensor')), may hold values from -6 to 6
- w_gate: bfloat16 [4096, 8192], P('seq', 'tensor'), may hold values from -0.09375 to 0.09375
- w_xin: bfloat16 [4096, 8192], P('seq', 'tensor'), may hold values from -0.09375 to 0.09375
- w_bc: bfloat16 [4096, 2048], P('seq', 'tensor'), may hold values from -0.09375 to 0.09375
- w_dt: bfloat16 [4096, 128], P('seq', 'tensor'), may hold values from -0.09375 to 0.09375
- conv_x: float32 [4, 8192], P(None, 'tensor'), may hold values from -3 to 3
- conv_x_bias: float32 [8192], P('tensor'), may hold values from -3 to 3
- conv_bc: float32 [4, 2048], P(None, 'tensor'), may hold values from -3 to 3
- conv_bc_bias: float32 [2048], P('tensor'), may hold values from -3 to 3
- dt_bias: float32 [128], P('tensor'), may hold values from -1 to 1
- decay_rate: float32 [128], P('tensor'), may hold values from 0.000390625 to 0.08, as said below
- d_skip: float32 [128], P('tensor'), may hold values from 0.5 to 1.5
- norm_gain: float32 [8192], P('tensor'), may hold values from 0.25 to 1.75
- w_out: bfloat16 [8192, 4096], P('tensor', 'seq'), may hold values from -0.0625 to 0.0625
- lengths: int32 [8], replicated, may hold values from 1 to 512, 1024 in all
Outputs:
- mixed: bfloat16 [1024, 4096], P(('seq', 'tensor'))
Inputs may be any that keep to these rules, and one draw needn't show every extreme that they name: lengths of 8 prompts that fill the pack of 1024 tokens exactly; the longest is exactly 512. `decay_rate`: positive rates.
All inputs are finite; a program needn't handle non-finite values.
Results may differ from a plain program's by a relative error of at most 0.03.
Values may be sent and summed in bfloat16 or wider, within the bound.
A program may use at most 64 MiB of HBM per device.

v0:
```python
import jax
import jax.numpy as jnp
import numpy as np
from jax import lax
from jax.sharding import PartitionSpec as P

HDIM = 64
GROUPS = 8
STATE = 128
CONV = 4
STRETCH = 256
INNER = 8192


HIGH = lax.Precision.HIGHEST


def from_behind(x, axis, by):
    count = lax.axis_size(axis)
    pairs = [(i, i + by) for i in range(count) if 0 <= i + by < count]
    return lax.ppermute(x, axis, pairs)


def carried_in(x, axis, combine, identity):
    count, here = (lax.axis_size(axis), lax.axis_index(axis))
    everything = jax.tree.map(
        lambda part, kind: lax.all_gather(part.astype(kind), axis), x, (jnp.bfloat16, jnp.bfloat16)
    )
    start = jax.tree.map(
        lambda part, zero: jnp.broadcast_to(jnp.asarray(zero, part.dtype), part.shape), x, identity
    )

    def hop(k, before):
        reached = k < here
        new = combine(
            before, jax.tree.map(lambda part, own: part[k].astype(own.dtype), everything, x)
        )
        return jax.tree.map(lambda a, b: jnp.where(reached, a, b), new, before)

    return lax.fori_loop(0, count, hop, start)


def doc_ids(lengths, positions):
    starts = jnp.cumsum(lengths) - lengths
    counted = jnp.sum((starts[None, :] <= positions[:, None]).astype(jnp.int32), axis=1)
    return counted - 1


def causal_conv(values, edge, weights, bias, docs, edge_docs):
    count = values.shape[0]
    extended = jnp.concatenate([edge, values], axis=0).astype(jnp.float32)
    all_docs = jnp.concatenate([edge_docs, docs])
    summed = jnp.zeros(values.shape, jnp.float32) + bias[None, :]
    for offset in range(weights.shape[0]):
        same = (all_docs[offset : offset + count] == docs).astype(jnp.float32)
        summed = (
            summed + weights[offset][None, :] * extended[offset : offset + count] * same[:, None]
        )
    return lax.optimization_barrier(jax.nn.silu(summed).astype(jnp.bfloat16))


def ssd_blocks(xvals, dtv, rate, bmat, cmat, docs, prev_doc, head_group, block):
    count, heads, hdim = xvals.shape
    nstate = bmat.shape[2]
    blocks = count // block
    logs = -dtv * rate[None, :]

    def split(array):
        return array.reshape((blocks, block) + array.shape[1:])

    lower = jnp.tril(jnp.ones((block, block), bool))

    def step(carry, pieces):
        state, last_doc = carry
        xblk, dblk, lblk, bblk, cblk, docblk = pieces
        cum = jnp.cumsum(lblk, axis=0)
        same = (docblk[:, None] == docblk[None, :]) & lower
        diff = cum.T[:, :, None] - cum.T[:, None, :]
        decay = jnp.exp(jnp.where(same[None], diff, -jnp.inf))
        scores = jnp.einsum("ign,jgn->gij", cblk, bblk, precision=HIGH)
        mixing = scores[head_group] * decay * dblk.T[:, None, :]
        inner = jnp.einsum("hij,jhp->ihp", mixing, xblk, precision=HIGH)
        open_in = (docblk == last_doc).astype(jnp.float32)
        carry_in = jnp.exp(cum) * open_in[:, None]
        chead = cblk[:, head_group, :]
        outer = jnp.einsum("ihn,hpn->ihp", chead, state, precision=HIGH) * carry_in[:, :, None]
        end_doc = docblk[-1]
        tail = (
            jnp.exp(cum[-1][None, :] - cum)
            * (docblk == end_doc).astype(jnp.float32)[:, None]
            * dblk
        )
        bhead = bblk[:, head_group, :]
        fresh = jnp.einsum("jh,jhp,jhn->hpn", tail, xblk, bhead, precision=HIGH)
        state = carry_in[-1][:, None, None] * state + fresh
        return ((state, end_doc), inner + outer)

    init = (jnp.zeros((heads, hdim, nstate), jnp.float32), prev_doc)
    (state, end_doc), outs = lax.scan(
        step, init, (split(xvals), split(dtv), split(logs), split(bmat), split(cmat), split(docs))
    )
    return (outs.reshape(count, heads, hdim), state)


def shards(
    tokens,
    w_gate,
    w_xin,
    w_bc,
    w_dt,
    conv_x,
    conv_x_bias,
    conv_bc,
    conv_bc_bias,
    dt_bias,
    decay_rate,
    d_skip,
    norm_gain,
    w_out,
    lengths,
):
    tensor_count = lax.axis_size("tensor")
    seq_index = lax.axis_index("seq")
    tensor_index = lax.axis_index("tensor")
    span_rows = lax.all_gather(tokens, "tensor", axis=0, tiled=True)
    span_len = span_rows.shape[0]
    pieces = (
        lax.all_gather(w_gate, "seq", axis=0, tiled=True),
        lax.all_gather(w_xin, "seq", axis=0, tiled=True),
        lax.all_gather(w_bc, "seq", axis=0, tiled=True),
        lax.all_gather(w_dt, "seq", axis=0, tiled=True),
    )
    gate_acc, xin_acc, bc_acc, dt_acc = tuple(
        (
            jnp.dot(span_rows, weight_piece, preferred_element_type=jnp.float32)
            for weight_piece in pieces
        )
    )
    gate = gate_acc.astype(jnp.bfloat16)
    xin = xin_acc.astype(jnp.bfloat16)
    bcin = bc_acc.astype(jnp.bfloat16)
    dtin = dt_acc.astype(jnp.bfloat16)
    gate, xin, bcin, dtin = lax.optimization_barrier((gate, xin, bcin, dtin))
    positions = seq_index * span_len + jnp.arange(span_len, dtype=jnp.int32)
    docs = doc_ids(lengths, positions)
    edge_docs = doc_ids(lengths, seq_index * span_len + jnp.arange(-(CONV - 1), 0, dtype=jnp.int32))
    prev_span_doc = doc_ids(lengths, positions[:1] - 1)[0]
    edge_x, edge_bc = from_behind(
        (xin[span_len - (CONV - 1) :], bcin[span_len - (CONV - 1) :]), "seq", 1
    )
    x_conv = causal_conv(xin, edge_x, conv_x, conv_x_bias, docs, edge_docs)
    bc_conv = causal_conv(bcin, edge_bc, conv_bc, conv_bc_bias, docs, edge_docs)
    group_span = tensor_count // GROUPS
    my_group = tensor_index // group_span
    every_group = lax.all_gather(bc_conv, "tensor", axis=1, tiled=True)
    arranged = every_group.reshape(span_len, 2 * STATE, GROUPS)
    group_cols = lax.dynamic_slice_in_dim(arranged, my_group, 1, 2).reshape(span_len, 2 * STATE)
    head_dev = w_dt.shape[1]
    head_group = np.zeros(head_dev, dtype=np.int32)
    both = group_cols.astype(jnp.float32)
    bmat = both[:, None, :STATE]
    cmat = both[:, None, STATE:]
    xvals = x_conv.astype(jnp.float32).reshape(span_len, head_dev, HDIM)
    dtv = jax.nn.softplus(dtin.astype(jnp.float32) + dt_bias[None, :])
    block = min(STRETCH, span_len)
    y_local, end_state = ssd_blocks(
        xvals, dtv, decay_rate, bmat, cmat, docs, prev_span_doc, head_group, block
    )
    cum_span = jnp.cumsum(-dtv * decay_rate[None, :], axis=0)
    open_span = (docs == prev_span_doc).astype(jnp.float32)
    span_decay = jnp.exp(cum_span[-1]) * open_span[-1]

    def combine(earlier, later):
        return (earlier[0] * later[0], later[0][:, None, None] * earlier[1] + later[1])

    entering = carried_in(
        (span_decay, end_state),
        "seq",
        combine,
        (jnp.ones_like(span_decay), jnp.zeros_like(end_state)),
    )[1]
    carried = jnp.exp(cum_span) * open_span[:, None]
    y_enter = (
        jnp.einsum("ihn,hpn->ihp", cmat[:, head_group, :], entering, precision=HIGH)
        * carried[:, :, None]
    )
    yvals = (y_local + y_enter + d_skip[None, :, None] * xvals).reshape(span_len, head_dev * HDIM)
    gated = yvals * jax.nn.silu(gate.astype(jnp.float32))
    local_sq = jnp.sum(gated * gated, axis=1)
    group_mark = (jnp.arange(GROUPS) == my_group).astype(jnp.float32)
    every_sum = lax.psum(local_sq[:, None] * group_mark[None, :], "tensor")
    group_mean = jnp.sum(every_sum * group_mark[None, :], axis=1) / (INNER // GROUPS)
    normed = (gated * lax.rsqrt(group_mean + 1e-05)[:, None] * norm_gain[None, :]).astype(
        jnp.bfloat16
    )
    w_full = lax.all_gather(w_out, "seq", axis=1, tiled=True)
    return lax.psum_scatter(
        jnp.dot(normed, w_full, preferred_element_type=jnp.float32).astype(jnp.bfloat16),
        "tensor",
        scatter_dimension=0,
        tiled=True,
    )


def solution(mesh):
    in_specs = (
        P(("seq", "tensor"), None),
        P("seq", "tensor"),
        P("seq", "tensor"),
        P("seq", "tensor"),
        P("seq", "tensor"),
        P(None, "tensor"),
        P("tensor"),
        P(None, "tensor"),
        P("tensor"),
        P("tensor"),
        P("tensor"),
        P("tensor"),
        P("tensor"),
        P("tensor", "seq"),
        P(),
    )
    out_specs = P(("seq", "tensor"), None)
    return jax.shard_map(shards, mesh=mesh, in_specs=in_specs, out_specs=out_specs, check_vma=False)
```

profile of v0, /device:TPU:0, one launch (start us, length us, event | category | flops | bytes accessed | tf_op | source)
XLA Modules:
  0.0 462.2 jit_solution(14876827878078978227)
XLA Ops:
  12.7 9.9 %all_gather.35 = bf16[4096,16]{0,1:T(8,128)(2,1)S(1)} all-gather(bf16[1024,16]{0,1:T(8,128)(2,1)S(1)} %copy-done.2), channel_id=1, replica_groups=mesh['seq'=4,'tensor'=8] {'seq'}, dimensions={0}, use_global_device_ids=true | all-gather | bytes 163840 | tf_op jit(solution)/shard_map/all_gather | solution.py:131
  22.9 17.9 %all-gather.10.cloned.1.call-done = bf16[256,4096]{1,0:T(8,128)(2,1)} async-done(((bf16[32,4096]{1,0:T(8,128)(2,1)}), bf16[256,4096]{1,0:T(8,128)(2,1)}) %all-gather.10.cloned.1.call-update) | async-done | bytes 2097168 | tf_op jit(solution)/shard_map/all_gather | solution.py:125
  40.8 2.4 convolution_convert_fusion.4
  43.2 34.3 %all-gather.16.cloned.1.call-done = bf16[4096,256]{1,0:T(8,128)(2,1)} async-done(((bf16[1024,256]{1,0:T(8,128)(2,1)}), bf16[4096,256]{1,0:T(8,128)(2,1)}) %all-gather.16.cloned.1.call-update) | async-done | bytes 2097168 | tf_op jit(solution)/shard_map/all_gather | solution.py:130
  77.5 2.3 convolution_convert_fusion.3
  79.8 87.1 %all-gather.12.cloned.1.call-done = bf16[4096,1024]{1,0:T(8,128)(2,1)} async-done(((bf16[1024,1024]{1,0:T(8,128)(2,1)}), bf16[4096,1024]{1,0:T(8,128)(2,1)}) %all-gather.12.cloned.1.call-update) | async-done | bytes 8388624 | tf_op jit(solution)/shard_map/all_gather | solution.py:128
  167.0 6.6 %convolution_convert_fusion.2 = bf16[256,1024]{1,0:T(8,128)(2,1)} fusion(bf16[256,4096]{1,0:T(8,128)(2,1)S(1)} %copy-done, bf16[4096,1024]{1,0:T(8,128)(2,1)} %all-gather.12.cloned.1.call-done), kind=kOutput, calls=%fused_computation.29 | convolution fusion | flops 2147745792 | bytes 11010048 | tf_op jit(solution)/shard_map/dot_general | solution.py:135
  173.5 82.8 %all-gather.14.cloned.1.call-done = bf16[4096,1024]{1,0:T(8,128)(2,1)} async-done(((bf16[1024,1024]{1,0:T(8,128)(2,1)}), bf16[4096,1024]{1,0:T(8,128)(2,1)}) %all-gather.14.cloned.1.call-update) | async-done | bytes 8388624 | tf_op jit(solution)/shard_map/all_gather | solution.py:129
  256.3 5.8 %convolution_convert_fusion.1 = bf16[256,1024]{1,0:T(8,128)(2,1)S(1)} fusion(bf16[256,4096]{1,0:T(8,128)(2,1)S(1)} %copy-done, bf16[4096,1024]{1,0:T(8,128)(2,1)} %all-gather.14.cloned.1.call-done), kind=kOutput, calls=%fused_computation.28 | convolution fusion | flops 2147745792 | bytes 11010048 | tf_op jit(solution)/shard_map/dot_general | solution.py:135
  262.1 3.4 collective-permute-start.1
  268.7 4.2 collective-permute-start
  275.5 18.1 %all-gather.18.cloned.1.call-done = bf16[256,2048]{1,0:T(8,128)(2,1)} async-done(((bf16[256,256]{1,0:T(8,128)(2,1)}), bf16[256,2048]{1,0:T(8,128)(2,1)}) %all-gather.18.cloned.1.call-update) | async-done | bytes 1048592 | tf_op jit(solution)/shard_map/all_gather | solution.py:155
  293.6 1.5 copy.39
  295.5 1.4 fusion.21
  299.2 7.2 %all-gather.1 = bf16[4,1,16]{2,1,0:T(2,128)(2,1)S(1)} all-gather(bf16[1,1,16]{2,1,0:T(2,128)(2,1)S(1)} %bitcast.101), channel_id=1, replica_groups=mesh['seq'=4,'tensor'=8] {'seq'}, dimensions={0}, use_global_device_ids=true | all-gather | bytes 160 | tf_op jit(solution)/shard_map/all_gather | solution.py:27
  306.5 3.2 fusion.13
  309.7 1.2 fusion.20
  310.9 11.6 %all-gather.22.cloned.1.call-done = bf16[64,64,128]{2,1,0:T(8,128)(2,1)} async-done(((bf16[16,64,128]{2,1,0:T(8,128)(2,1)}), bf16[64,64,128]{2,1,0:T(8,128)(2,1)}) %all-gather.22.cloned.1.call-update) | async-done | bytes 1048592 | tf_op jit(solution)/shard_map/all_gather | solution.py:27
  322.6 4.5 while.9
  327.1 1.3 fusion.18
  329.9 16.6 %psum.7 = f32[256,8]{0,1:T(8,128)S(1)} all-reduce(f32[256,8]{0,1:T(8,128)S(1)} %broadcast_multiply_fusion), channel_id=1, replica_groups=mesh['seq'=4,'tensor'=8] {'tensor'}, use_global_device_ids=true, to_apply=%region_9.10 | all-reduce | flops 2048 | bytes 16384 | tf_op jit(solution)/shard_map/psum | solution.py:191
  346.6 65.5 %all-gather.20.cloned.1.call-done = bf16[1024,4096]{1,0:T(8,128)(2,1)} async-done(((bf16[1024,1024]{1,0:T(8,128)(2,1)}), bf16[1024,4096]{1,0:T(8,128)(2,1)}) %all-gather.20.cloned.1.call-update) | async-done | bytes 8388624 | tf_op jit(solution)/shard_map/all_gather | solution.py:196
  412.1 7.3 %convolution_convert_fusion = bf16[256,4096]{1,0:T(8,128)(2,1)} fusion(bf16[1024,4096]{1,0:T(8,128)(2,1)} %all-gather.20.cloned.1.call-done, f32[1024]{0:T(1024)S(1)} %copy-done.11, f32[256]{0:T(256)S(1)} %add_rsqrt_fusion, f32[256,1024]{1,0:T(8,128)S(1)} %copy.43, bf16[256,1024]{1,0:T(8,128)(2,1)S(1)} %copy-done.1), kind=kOutput, calls=%fused_computation.3 | convolution fusion | flops 2150891520 | bytes 12063744 | tf_op jit(solution)/shard_map/dot_general | solution.py:198
  419.4 36.0 %reduce-scatter.2.cloned.1.call-done = bf16[32,4096]{1,0:T(8,128)(2,1)} async-done(((bf16[256,4096]{1,0:T(8,128)(2,1)}), bf16[32,4096]{1,0:T(8,128)(2,1)}) %reduce-scatter.2.cloned.1.call-update) | async-done | bytes 262160 | tf_op jit(solution)/shard_map/reduce_scatter | solution.py:197
  (95 shorter events, 19.7 us)
Async XLA Ops:
  6.5 34.3 %all-gather.10.cloned.1.call-start = ((), (), s32[]{:S(2)}) async-start(), calls=%async_computation.1 | async-start | bytes 2359296 | tf_op jit(solution)/shard_map/all_gather | solution.py:125
  7.3 70.2 %all-gather.16.cloned.1.call-start = ((), (), s32[]{:S(2)}) async-start(), calls=%async_computation.4 | async-start | bytes 2621440 | tf_op jit(solution)/shard_map/all_gather | solution.py:130
  8.0 1.9 copy-start.8
  8.0 4.7 %copy-start.2 = (bf16[1024,16]{0,1:T(8,128)(2,1)S(1)}, bf16[1024,16]{0,1:T(8,128)(2,1)}, u32[]{:S(2)}) copy-start(bf16[1024,16]{0,1:T(8,128)(2,1)} %param.26) | copy-start | bytes 98308
  8.0 14.9 %copy-start.4 = (f32[4,256]{1,0:T(4,128)S(1)}, f32[4,256]{1,0:T(4,128)}, u32[]{:S(2)}) copy-start(f32[4,256]{1,0:T(4,128)} %param.29) | copy-start | bytes 12292
  8.0 158.9 %all-gather.12.cloned.1.call-start = ((), (), s32[]{:S(2)}) async-start(), calls=%async_computation.2 | async-start | bytes 10485760 | tf_op jit(solution)/shard_map/all_gather | solution.py:128
  8.8 247.5 %all-gather.14.cloned.1.call-start = ((), (), s32[]{:S(2)}) async-start(), calls=%async_computation.3 | async-start | bytes 10485760 | tf_op jit(solution)/shard_map/all_gather | solution.py:129
  9.3 284.2 %all-gather.18.cloned.1.call-start = ((), (), s32[]{:S(2)}) async-start(), calls=%async_computation.5 | async-start | bytes 1179648 | tf_op jit(solution)/shard_map/all_gather | solution.py:155
  40.8 36.7 %copy-start = (bf16[256,4096]{1,0:T(8,128)(2,1)S(1)}, bf16[256,4096]{1,0:T(8,128)(2,1)}, u32[]{:S(2)}) copy-start(bf16[256,4096]{1,0:T(8,128)(2,1)} %all-gather.10.cloned.1.call-done) | copy-start | bytes 6291460
  173.5 93.3 %copy-start.7 = (f32[256]{0:T(256)S(1)}, f32[256]{0:T(256)}, u32[]{:S(2)}) copy-start(f32[256]{0:T(256)} %param.30) | copy-start | bytes 3076
  173.5 94.3 %copy-start.3 = (f32[4,1024]{1,0:T(4,128)S(1)}, f32[4,1024]{1,0:T(4,128)}, u32[]{:S(2)}) copy-start(f32[4,1024]{1,0:T(4,128)} %param.27) | copy-start | bytes 49156
  173.5 94.3 %copy-start.6 = (f32[16]{0:T(128)S(1)}, f32[16]{0:T(128)}, u32[]{:S(2)}) copy-start(f32[16]{0:T(128)} %param.31) | copy-start | bytes 196
  173.5 94.3 %copy-start.9 = (f32[16]{0:T(128)S(1)}, f32[16]{0:T(128)}, u32[]{:S(2)}) copy-start(f32[16]{0:T(128)} %param.32) | copy-start | bytes 196
  262.1 12.4 %copy-start.5 = (f32[1024]{0:T(1024)S(1)}, f32[1024]{0:T(1024)}, u32[]{:S(2)}) copy-start(f32[1024]{0:T(1024)} %param.28) | copy-start | bytes 12292
  262.1 4.7 %collective-permute-start.1 = (bf16[3,256]{1,0:T(4,128)(2,1)S(1)}, bf16[3,256]{1,0:T(4,128)(2,1)S(1)}, u32[]{:S(2)}, u32[]{:S(2)}) collective-permute-start(bf16[3,256]{1,0:T(4,128)(2,1)S(1)} %slice.112), channel_id=1, source_target_pairs={{0,8},{8,16},{16,24},{1,9},{9,17},{17,25},{2,10},{10,18},{18,26},{... | collective-permute-start | bytes 4616 | tf_op jit(solution)/shard_map/ppermute | solution.py:21
  267.7 54.8 %all-gather.22.cloned.1.call-start = ((), (), s32[]{:S(2)}) async-start(), calls=%async_computation.8 | async-start | bytes 1310720 | tf_op jit(solution)/shard_map/all_gather | solution.py:27
  268.7 5.5 %collective-permute-start = (bf16[3,1024]{1,0:T(4,128)(2,1)S(1)}, bf16[3,1024]{1,0:T(4,128)(2,1)S(1)}, u32[]{:S(2)}, u32[]{:S(2)}) collective-permute-start(bf16[3,1024]{1,0:T(4,128)(2,1)S(1)} %slice.100), channel_id=1, source_target_pairs={{0,8},{8,16},{16,24},{1,9},{9,17},{17,25},{2,10},{10,18},{18,26},{... | collective-permute-start | bytes 18440 | tf_op jit(solution)/shard_map/ppermute | solution.py:21
  296.9 115.1 %all-gather.20.cloned.1.call-start = ((), (), s32[]{:S(2)}) async-start(), calls=%async_computation.6 | async-start | bytes 10485760 | tf_op jit(solution)/shard_map/all_gather | solution.py:196
  297.7 157.7 %reduce-scatter.2.cloned.1.call-start = ((), (), s32[]{:S(2)}) async-start(), calls=%async_computation.7 | async-start | bytes 2359296 | tf_op jit(solution)/shard_map/reduce_scatter | solution.py:197
  322.6 4.5 copy-start.10
  328.4 1.0 copy-start.1
  328.4 83.7 %copy-start.11 = (f32[1024]{0:T(1024)S(1)}, f32[1024]{0:T(1024)}, u32[]{:S(2)}) copy-start(f32[1024]{0:T(1024)} %param.34) | copy-start | bytes 12292
Sparse Core Ops, SparseCore 0:
  9.0 31.7 all-gather.9
  42.6 34.7 all-gather.15
  79.3 87.5 all-gather.11
  168.7 87.5 all-gather.13
  267.9 25.6 all-gather.17
  297.0 25.4 all-gather.21
  324.4 87.5 all-gather.19
  419.5 35.7 reduce-scatter.1
where the time goes:
time: 463 us; the launch traced here: 462 us
  waiting for transfers between devices  358 us (77%)
  blocking collectives  33.7 us (7%)
  matrix products  31.6 us (7%)
  between operations  15.1 us (3%)
  other arithmetic  10.7 us (2%)
  starting transfers between devices  7.82 us (2%)
  local copies, waits for them, and re-layouts  5.23 us (1%)
    all_gather x1, waiting for transfers between devices, shards(): lax.all_gather(w_gate, 'seq', axis=0, tiled=True)  87.1 us
    all_gather x1, waiting for transfers between devices, shards(): lax.all_gather(w_xin, 'seq', axis=0, tiled=True)  82.8 us
    all_gather x1, waiting for transfers between devices, shards(): w_full = lax.all_gather(w_out, 'seq', axis=1, tiled=True)  65.5 us
    reduce_scatter x1, waiting for transfers between devices, shards(): lax.psum_scatter(jnp.dot(normed, w_full, preferred_element_type=jnp.float...  36 us
    all_gather x1, waiting for transfers between devices, shards(): lax.all_gather(w_bc, 'seq', axis=0, tiled=True)  34.3 us
    all_gather x1, waiting for transfers between devices, shards(): every_group = lax.all_gather(bc_conv, 'tensor', axis=1, tiled=True)  18.1 us
    all_gather x1, waiting for transfers between devices, shards(): span_rows = lax.all_gather(tokens, 'tensor', axis=0, tiled=True)  17.9 us
    dot_general x4, matrix products, shards(): jnp.dot(span_rows, weight_piece, preferred_element_type=jnp.float32)  17 us
  transfers between devices with their start and end apart: 10, of which 10 were waited for; matrix products, arithmetic and copies ran while one was open for 6% of the time, Pallas kernels for 0%

commit v1 on v0

--- a/solution.py
+++ b/solution.py
@@ -102,7 +102,7 @@
     return (outs.reshape(count, heads, hdim), state)
 
 
-def shards(
+def shards_wide(
     tokens,
     w_gate,
     w_xin,
@@ -202,7 +202,142 @@
     )
 
 
+def conv_full(values, weights, bias, docs, axis):
+    count = values.shape[axis]
+    values = values.astype(jnp.float32)
+
+    def along(vector):
+        return vector[:, None] if axis == 0 else vector[None, :]
+
+    def across(vector):
+        return vector[None, :] if axis == 0 else vector[:, None]
+
+    summed = across(weights[CONV - 1]) * values + across(bias)
+    for back in range(1, CONV):
+        kept = lax.slice_in_dim(values, 0, count - back, axis=axis)
+        pad = [(0, 0), (0, 0)]
+        pad[axis] = (back, 0)
+        same = jnp.concatenate(
+            [jnp.zeros((back,), jnp.float32), (docs[:-back] == docs[back:]).astype(jnp.float32)]
+        )
+        summed = summed + across(weights[CONV - 1 - back]) * jnp.pad(kept, pad) * along(same)
+    return jax.nn.silu(summed).astype(jnp.bfloat16)
+
+
+def scan_heads(xc, dtv, rate, bmat, cmat, docs, block):
+    count, heads = dtv.shape
+    blocks = count // block
+    xh = xc.reshape(blocks, block, heads, HDIM)
+    dtb = dtv.reshape(blocks, block, heads)
+    cum = jnp.cumsum(-dtb * rate[None, None, :], axis=1)
+    docb = docs.reshape(blocks, block)
+    bb = bmat.reshape(STATE, blocks, block)
+    cb = cmat.reshape(STATE, blocks, block)
+    scores = jnp.einsum("nbi,nbj->bij", cb, bb, preferred_element_type=jnp.float32)
+    lower = jnp.tril(jnp.ones((block, block), bool))
+    same = (docb[:, :, None] == docb[:, None, :]) & lower[None]
+    cumt = cum.transpose(0, 2, 1)
+    diff = cumt[:, :, :, None] - cumt[:, :, None, :]
+    decay = jnp.exp(jnp.where(same[:, None], diff, -jnp.inf))
+    mixing = scores[:, None] * decay * dtb.transpose(0, 2, 1)[:, :, None, :]
+    inner = jnp.einsum(
+        "bhij,bjhp->bihp", mixing.astype(jnp.bfloat16), xh, preferred_element_type=jnp.float32
+    )
+    end_doc = docb[:, -1]
+    last_doc = jnp.concatenate([jnp.full((1,), -1, docs.dtype), end_doc[:-1]])
+    carry_in = jnp.exp(cum) * (docb == last_doc[:, None]).astype(jnp.float32)[:, :, None]
+    tail = jnp.exp(cum[:, -1:] - cum) * (docb == end_doc[:, None]).astype(jnp.float32)[:, :, None] * dtb
+    tx = (tail[..., None] * xh.astype(jnp.float32)).astype(jnp.bfloat16)
+    fresh = jnp.einsum("bjhp,nbj->bhpn", tx, bb, preferred_element_type=jnp.float32)
+    states = [jnp.zeros((heads, HDIM, STATE), jnp.float32)]
+    for k in range(blocks - 1):
+        states.append(carry_in[k, -1][:, None, None] * states[-1] + fresh[k])
+    entering = jnp.stack(states).astype(jnp.bfloat16)
+    outer = jnp.einsum("nbi,bhpn->bihp", cb, entering, preferred_element_type=jnp.float32)
+    return (inner + outer * carry_in[..., None]).reshape(count, heads * HDIM)
+
+
+def shards(
+    tokens,
+    w_gate,
+    w_xin,
+    w_bc,
+    w_dt,
+    conv_x,
+    conv_x_bias,
+    conv_bc,
+    conv_bc_bias,
+    dt_bias,
+    decay_rate,
+    d_skip,
+    norm_gain,
+    w_out,
+    lengths,
+):
+    seqs = lax.axis_size("seq")
+    tens = lax.axis_size("tensor")
+    here = lax.axis_index("seq")
+    own, depth = tokens.shape[0], w_gate.shape[0]
+    total = own * seqs * tens
+    chans = w_gate.shape[1] // seqs
+    heads = w_dt.shape[1] // seqs
+    parts = w_bc.shape[1] // (seqs * GROUPS)
+    columns = lax.all_to_all(tokens, "seq", 1, 0, tiled=True)
+    rows = lax.all_gather(columns, "tensor", axis=0)
+    rows = rows.reshape(tens, seqs, own, depth).transpose(1, 0, 2, 3).reshape(total, depth)
+
+    def project(weight):
+        return jnp.dot(rows, weight, preferred_element_type=jnp.float32).astype(jnp.bfloat16)
+
+    gate = lax.psum_scatter(project(w_gate), "seq", scatter_dimension=1, tiled=True)
+    xin = lax.psum_scatter(project(w_xin), "seq", scatter_dimension=1, tiled=True)
+    small = jnp.concatenate(
+        [
+            w_bc.T.reshape(seqs, parts, GROUPS, depth)
+            .transpose(0, 2, 1, 3)
+            .reshape(seqs, parts * GROUPS, depth),
+            w_dt.T.reshape(seqs, heads, depth),
+        ],
+        axis=1,
+    )
+    small = jnp.einsum("scd,td->sct", small, rows, preferred_element_type=jnp.float32)
+    small = lax.psum_scatter(small.astype(jnp.bfloat16), "seq", scatter_dimension=0, tiled=True)[0]
+    docs = doc_ids(lengths, jnp.arange(total, dtype=jnp.int32))
+
+    def mine(vector, width, axis=0):
+        return lax.dynamic_slice_in_dim(vector, here * width, width, axis)
+
+    xc = conv_full(xin, mine(conv_x, chans, 1), mine(conv_x_bias, chans), docs, 0)
+
+    def grouped(vector):
+        lead = vector.shape[:-1]
+        vector = mine(vector, parts * GROUPS, len(lead)).reshape(lead + (parts, GROUPS))
+        return jnp.swapaxes(vector, -1, -2).reshape(lead + (parts * GROUPS,))
+
+    bcc = conv_full(small[: parts * GROUPS], grouped(conv_bc), grouped(conv_bc_bias), docs, 1)
+    bcc = lax.all_to_all(bcc.reshape(GROUPS, parts, total), "tensor", 0, 0, tiled=True)
+    bcc = lax.all_gather(bcc, "seq", axis=0).transpose(1, 0, 2, 3).reshape(2 * STATE, total)
+    dtin = small[parts * GROUPS :].T.astype(jnp.float32)
+    dtv = jax.nn.softplus(dtin + mine(dt_bias, heads)[None, :])
+    y = scan_heads(
+        xc, dtv, mine(decay_rate, heads), bcc[:STATE], bcc[STATE:], docs, min(STRETCH, total)
+    )
+    y = y + jnp.repeat(mine(d_skip, heads), HDIM)[None, :] * xc.astype(jnp.float32)
+    gated = (y * jax.nn.silu(gate.astype(jnp.float32))).astype(jnp.bfloat16)
+    gated = lax.all_gather(gated, "seq", axis=1, tiled=True).astype(jnp.float32)
+    mean = jnp.mean(gated * gated, axis=1, keepdims=True)
+    normed = (gated * lax.rsqrt(mean + 1e-05) * norm_gain[None, :]).astype(jnp.bfloat16)
+    out = jnp.dot(normed, w_out, preferred_element_type=jnp.float32).astype(jnp.bfloat16)
+    out = out.reshape(seqs, tens, own, depth).transpose(1, 0, 2, 3)
+    out = lax.psum_scatter(out, "tensor", scatter_dimension=0, tiled=True)[0]
+    return lax.all_to_all(out, "seq", 0, 2, tiled=True)[0]
+
+
 def solution(mesh):
+    seqs, tens = mesh.shape["seq"], mesh.shape["tensor"]
+    heads = INNER // HDIM
+    narrow = tens == GROUPS and heads % (seqs * tens) == 0 and 2 * STATE % (seqs * tens) == 0
+    body = shards if narrow else shards_wide
     in_specs = (
         P(("seq", "tensor"), None),
         P("seq", "tensor"),
@@ -221,4 +356,4 @@
         P(),
     )
     out_specs = P(("seq", "tensor"), None)
-    return jax.shard_map(shards, mesh=mesh, in_specs=in_specs, out_specs=out_specs, check_vma=False)
+    return jax.shard_map(body, mesh=mesh, in_specs=in_specs, out_specs=out_specs, check_vma=False)

time: 463 us -> 305 us (0.66)
  waiting for transfers between devices: 358 us -> 184 us
  local copies, waits for them, and re-layouts: 5.23 us -> 26.5 us
  matrix products: 31.6 us -> 22.9 us
  other arithmetic: 10.7 us -> 19.3 us
    all_gather x7 -> x2, waiting for transfers between devices: 317 us -> 61.9 us  [the longest x1 35.3 us: shards(): gated = lax.all_gather(gated, 'seq', axis=1, tiled=True).astype(jnp.float32)]
    unnamed x8, waiting for transfers between devices: 3.35 us -> 92.6 us
    all_to_all x0 -> x2, blocking collectives: none -> 20 us  [the longest x1 10.8 us: shards(): columns = lax.all_to_all(tokens, 'seq', 1, 0, tiled=True)]
    psum x1 -> x0, blocking collectives: 16.6 us -> none  [shards(): every_sum = lax.psum(local_sq[:, None] * group_mark[None, :], 'tensor')]
    reduce_scatter x1 -> x2, waiting for transfers between devices: 36 us -> 23.5 us  [the longest x1 20.2 us: shards(): lax.psum_scatter(project(w_gate), 'seq', scatter_dimension=1, tiled=True)]
    reshape x1 -> x8, local copies, waits for them, and re-layouts: 0.33 us -> 9.5 us  [the longest x2 5.96 us: scan_heads(): return (inner + outer * carry_in[..., None]).reshape(count, heads * HDIM)]
    dot_general x10 -> x8, matrix products: 31.6 us -> 22.9 us  [the longest x2 11.1 us: project(): jnp.dot(rows, weight, preferred_element_type=jnp.float32)]
    ppermute x2 -> x0, starting transfers between devices: 7.55 us -> none  [from_behind(): return lax.ppermute(x, axis, pairs)]
  transfers between devices with their start and end apart: 10 -> 7, of which waited for: 10 -> 7; matrix products, arithmetic and copies ran while one was open for 6% -> 16% of each run, Pallas kernels for 0% -> 0%
where the time goes in v1:
time: 305 us; the launch traced here: 304 us
  waiting for transfers between devices  184 us (60%)
  blocking collectives  32.2 us (11%)
  local copies, waits for them, and re-layouts  26.5 us (9%)
  matrix products  22.9 us (8%)
  other arithmetic  19.3 us (6%)
  between operations  13.8 us (5%)
  starting transfers between devices  4.8 us (2%)
    unnamed x8, waiting for transfers between devices  92.6 us
    all_gather x1, waiting for transfers between devices, shards(): gated = lax.all_gather(gated, 'seq', axis=1, tiled=True).astype(jnp.float32)  35.3 us
    all_gather x1, waiting for transfers between devices, shards(): rows = lax.all_gather(columns, 'tensor', axis=0)  26.6 us
    reduce_scatter x1, waiting for transfers between devices, shards(): lax.psum_scatter(project(w_gate), 'seq', scatter_dimension=1, tiled=True)  20.2 us
    all_gather x1, blocking collectives, shards(): lax.all_gather(bcc, 'seq', axis=0).transpose(1, 0, 2, 3)  12.2 us
    dot_general x2, matrix products, project(): jnp.dot(rows, weight, preferred_element_type=jnp.float32)  11.1 us
    all_to_all x1, blocking collectives, shards(): columns = lax.all_to_all(tokens, 'seq', 1, 0, tiled=True)  10.8 us
    all_to_all x1, blocking collectives, shards(): return lax.all_to_all(out, 'seq', 0, 2, tiled=True)[0]  9.17 us
  transfers between devices with their start and end apart: 7, of which 7 were waited for; matrix products, arithmetic and copies ran while one was open for 16% of the time, Pallas kernels for 0%

profile of v1, /device:TPU:0, one launch (start us, length us, event | category | flops | bytes accessed | tf_op | source)
XLA Modules:
  0.0 303.7 jit_solution(4885133332877469587)
XLA Ops:
  7.7 10.8 %all_to_all.36 = bf16[32,4,1024]{2,0,1:T(8,128)(2,1)} all-to-all(bf16[32,4,1024]{2,0,1:T(8,128)(2,1)S(1)} %bitcast.133), channel_id=1, replica_groups=mesh['seq'=4,'tensor'=8] {'seq'}, dimensions={1} | all-to-all | bytes 524288 | tf_op jit(solution)/shard_map/all_to_all | solution.py:285
  20.9 26.6 %all-gather.4.cloned.1.call-done = bf16[8,128,1024]{2,1,0:T(8,128)(2,1)} async-done(((bf16[1,128,1024]{2,1,0:T(8,128)(2,1)}), bf16[8,128,1024]{2,1,0:T(8,128)(2,1)}) %all-gather.4.cloned.1.call-update) | async-done | bytes 2097168 | tf_op jit(solution)/shard_map/all_gather | solution.py:286
  47.5 1.8 copy.198
  50.6 1.7 convolution_convert_fusion.2
  52.3 5.2 %convolution_convert_fusion.1 = bf16[1024,1024]{1,0:T(8,128)(2,1)} fusion(bf16[1024,1024]{1,0:T(8,128)(2,1)} %bitcast.125, bf16[1024,1024]{1,0:T(8,128)(2,1)S(1)} %copy-done), kind=kOutput, calls=%fused_computation.18 | convolution fusion | flops 2148532224 | bytes 6291456 | tf_op jit(solution)/shard_map/dot_general | solution.py:290
  63.3 5.9 %convolution_convert_fusion = bf16[1024,1024]{1,0:T(8,128)(2,1)} fusion(bf16[1024,1024]{1,0:T(8,128)(2,1)} %bitcast.126, bf16[1024,1024]{1,0:T(8,128)(2,1)} %param.16), kind=kOutput, calls=%fused_computation.17 | convolution fusion | flops 2148532224 | bytes 6291456 | tf_op jit(solution)/shard_map/dot_general | solution.py:290
  69.3 28.7 %all-reduce.13.cloned.1.call-done = bf16[4,68,1024]{2,1,0:T(8,128)(2,1)} async-done(((bf16[4,68,1024]{2,1,0:T(8,128)(2,1)}), bf16[4,68,1024]{2,1,0:T(8,128)(2,1)}) %all-reduce.13.cloned.1.call-update) | async-done | bytes 557072
  99.5 4.8 %reduce-window.20 = f32[4,4,2,128]{3,2,1,0:T(2,128)S(1)} reduce-window(f32[4,4,2,128]{3,2,1,0:T(2,128)S(1)} %reshape.237, f32[]{:T(128)} %constant.22.clone.1), window={size=1x1x1x128 pad=0_0x0_0x0_0x127_0}, to_apply=%region_4.5 | reduce-window | flops 520192 | bytes 32772 | tf_op jit(solution)/shard_map/reduce-window.1
  106.2 2.5 fusion.44
  108.7 4.6 %all-to-all-start.1 = ((bf16[8,8,1024]{2,1,0:T(8,128)(2,1)}), bf16[8,8,1024]{2,1,0:T(8,128)(2,1)S(1)}, u32[]{:S(2)}, u32[]{:S(2)}) async-start(bf16[8,8,1024]{2,1,0:T(8,128)(2,1)} %fusion.44), calls=%async_computation.2 | async-start | bytes 262144 | tf_op jit(solution)/shard_map/all_to_all | solution.py:318
  113.8 6.3 %all-to-all-done.1 = bf16[8,8,1024]{2,1,0:T(8,128)(2,1)S(1)} async-done(((bf16[8,8,1024]{2,1,0:T(8,128)(2,1)}), bf16[8,8,1024]{2,1,0:T(8,128)(2,1)S(1)}, u32[]{:S(2)}, u32[]{:S(2)}) %all-to-all-start.1) | async-done | bytes 131104 | tf_op jit(solution)/shard_map/all_to_all | solution.py:318
  120.1 12.2 %all-gather = bf16[32,8,1024]{2,1,0:T(8,128)(2,1)S(1)} all-gather(bf16[8,8,1024]{2,1,0:T(8,128)(2,1)S(1)} %all-to-all-done.1), channel_id=2, replica_groups=mesh['seq'=4,'tensor'=8] {'seq'}, dimensions={0}, use_global_device_ids=true | all-gather | bytes 655360 | tf_op jit(solution)/shard_map/all_gather | solution.py:319
  134.1 3.3 %reduce-scatter.6.cloned.1.call-done = bf16[1024,256]{1,0:T(8,128)(2,1)} async-done(((bf16[1024,1024]{1,0:T(8,128)(2,1)}), bf16[1024,256]{1,0:T(8,128)(2,1)}) %reduce-scatter.6.cloned.1.call-update) | async-done | bytes 524304 | tf_op jit(solution)/shard_map/reduce_scatter | solution.py:293
  141.1 2.2 reshape.227
  145.1 1.9 fusion.17
  148.4 2.7 copy.227
  151.1 3.2 %reshape.247 = f32[1024,256]{1,0:T(8,128)} reshape(f32[4,256,4,64]{3,2,1,0:T(4,128)} %copy.227) | data formatting | bytes 2097152 | tf_op jit(solution)/shard_map/reshape | solution.py:257
  154.4 20.2 %reduce-scatter.8.cloned.1.call-done = bf16[1024,256]{1,0:T(8,128)(2,1)} async-done(((bf16[1024,1024]{1,0:T(8,128)(2,1)}), bf16[1024,256]{1,0:T(8,128)(2,1)}) %reduce-scatter.8.cloned.1.call-update) | async-done | bytes 524304 | tf_op jit(solution)/shard_map/reduce_scatter | solution.py:292
  174.6 2.6 fusion.23
  177.2 35.3 %all-gather.6.cloned.1.call-done = bf16[1024,1024]{1,0:T(8,128)(2,1)} async-done(((bf16[1024,256]{1,0:T(8,128)(2,1)}), bf16[1024,1024]{1,0:T(8,128)(2,1)}) %all-gather.6.cloned.1.call-update) | async-done | bytes 2097168 | tf_op jit(solution)/shard_map/all_gather | solution.py:327
  212.5 2.2 fusion
  214.7 5.3 %fusion.14 = bf16[1024,1024]{1,0:T(8,128)(2,1)} fusion(bf16[1024,1024]{1,0:T(8,128)(2,1)} %param.28, bf16[1024,1024]{1,0:T(8,128)(2,1)S(1)} %copy-done.3, f32[1024]{0:T(1024)S(1)} %copy-done.7, f32[1024]{0:T(1024)S(1)} %add_rsqrt_fusion), kind=kOutput, calls=%fused_computation.16 | convolution fusion | flops 2152726528 | bytes 6299648 | tf_op jit(solution)/shard_map/dot_general | solution.py:330
  221.2 63.9 %all-reduce.15.cloned.1.call-done = bf16[8,4,32,1024]{3,2,0,1:T(8,128)(2,1)} async-done(((bf16[8,4,32,1024]{3,2,0,1:T(8,128)(2,1)}), bf16[8,4,32,1024]{3,2,0,1:T(8,128)(2,1)}) %all-reduce.15.cloned.1.call-update) | async-done | bytes 2097168
  286.7 9.2 %all_to_all.37 = bf16[4,32,1024]{2,1,0:T(8,128)(2,1)S(1)} all-to-all(bf16[4,32,1024]{2,1,0:T(8,128)(2,1)S(1)} %dynamic-slice_bitcast_fusion), channel_id=1, replica_groups=mesh['seq'=4,'tensor'=8] {'seq'}, dimensions={0} | all-to-all | bytes 524288 | tf_op jit(solution)/shard_map/all_to_all | solution.py:333
  (121 shorter events, 27.0 us)
Async XLA Ops:
  6.5 45.7 %copy-start = (bf16[1024,1024]{1,0:T(8,128)(2,1)S(1)}, bf16[1024,1024]{1,0:T(8,128)(2,1)}, u32[]{:S(2)}) copy-start(bf16[1024,1024]{1,0:T(8,128)(2,1)} %param.17) | copy-start | bytes 6291460
  6.5 40.9 %all-gather.4.cloned.1.call-start = ((), (), s32[]{:S(2)}) async-start(), calls=%async_computation.5 | async-start | bytes 2359296 | tf_op jit(solution)/shard_map/all_gather | solution.py:286
  18.5 79.5 %all-reduce.13.cloned.1.call-start = ((), (), s32[]{:S(2)}) async-start(), calls=%async_computation.9 | async-start | bytes 1179648
  49.2 1.3 copy-start.2
  52.2 85.1 %reduce-scatter.6.cloned.1.call-start = ((), (), s32[]{:S(2)}) async-start(), calls=%async_computation.6 | async-start | bytes 2621440 | tf_op jit(solution)/shard_map/reduce_scatter | solution.py:293
  57.5 0.7 copy-start.9
  57.5 0.7 copy-start.10
  57.5 0.8 copy-start.11
  57.5 1.0 copy-start.6
  57.5 1.6 copy-start.8
  57.5 2.2 copy-start.12
  57.5 2.4 copy-start.14
  57.6 117.0 %reduce-scatter.8.cloned.1.call-start = ((), (), s32[]{:S(2)}) async-start(), calls=%async_computation.7 | async-start | bytes 2621440 | tf_op jit(solution)/shard_map/reduce_scatter | solution.py:292
  108.7 11.4 %all-to-all-start.1 = ((bf16[8,8,1024]{2,1,0:T(8,128)(2,1)}), bf16[8,8,1024]{2,1,0:T(8,128)(2,1)S(1)}, u32[]{:S(2)}, u32[]{:S(2)}) async-start(bf16[8,8,1024]{2,1,0:T(8,128)(2,1)} %fusion.44), calls=%async_computation.2 | async-start | bytes 262144 | tf_op jit(solution)/shard_map/all_to_all | solution.py:318
  113.3 99.2 %all-gather.6.cloned.1.call-start = ((), (), s32[]{:S(2)}) async-start(), calls=%async_computation.8 | async-start | bytes 2621440 | tf_op jit(solution)/shard_map/all_gather | solution.py:327
  137.4 1.2 copy-start.1
  143.3 1.8 copy-start.4
  143.3 1.8 copy-start.5
  154.4 60.3 %copy-start.7 = (f32[1024]{0:T(1024)S(1)}, f32[1024]{0:T(1024)}, u32[]{:S(2)}) copy-start(f32[1024]{0:T(1024)} %param.27) | copy-start | bytes 12292
  177.1 107.9 %all-reduce.15.cloned.1.call-start = ((), (), s32[]{:S(2)}) async-start(), calls=%async_computation.10 | async-start | bytes 4194304
  212.5 2.2 copy-start.3
  220.0 0.7 copy-start.13
Sparse Core Ops, SparseCore 0:
  18.6 28.8 all-gather.3
  52.3 45.6 all-reduce.12
  101.2 36.0 reduce-scatter.5
  140.2 34.3 reduce-scatter.7
  177.3 35.1 all-gather.5
  220.1 64.9 all-reduce.14

commit v2 on v1

--- a/solution.py
+++ b/solution.py
@@ -2,6 +2,8 @@
 import jax.numpy as jnp
 import numpy as np
 from jax import lax
+from jax.experimental import pallas as pl
+from jax.experimental.pallas import tpu as pltpu
 from jax.sharding import PartitionSpec as P
 
 HDIM = 64
@@ -202,6 +204,291 @@
     )
 
 
+def enter(peers):
+    barrier = pltpu.get_barrier_semaphore()
+    for peer in peers:
+        pl.semaphore_signal(barrier, inc=1, device_id=peer, device_id_type=pl.DeviceIdType.MESH)
+    pl.semaphore_wait(barrier, len(peers))
+
+
+def remote(src, dst, send, recv, peer):
+    return pltpu.make_async_remote_copy(
+        src_ref=src,
+        dst_ref=dst,
+        send_sem=send,
+        recv_sem=recv,
+        device_id=peer,
+        device_id_type=pl.DeviceIdType.MESH,
+    )
+
+
+def places():
+    s, t = lax.axis_index("seq"), lax.axis_index("tensor")
+    seqs, chips = lax.axis_size("seq"), lax.axis_size("tensor") // 2
+    z, c = t // 2, t % 2
+
+    def along(ds, dz):
+        return lax.rem(s + ds, seqs), lax.rem(z + dz, chips)
+
+    return s, z, c, seqs, chips, along
+
+
+def out_kernel(
+    g_ref, gain_ref, w_ref, out_ref, held, normed, part, sib, pair, got,
+    g_send, g_recv, p_send, p_recv, o_send, o_recv,
+):
+    s, z, c, seqs, chips, along = places()
+    span = g_ref.shape[0] // seqs
+    width = g_ref.shape[1]
+    own = out_ref.shape[0]
+    cols = w_ref.shape[1]
+    sibling = (s, 2 * z + 1 - c)
+    offsets = [(ds, dz) for ds in range(seqs) for dz in range(chips) if ds or dz]
+    enter([(along(ds, dz)[0], 2 * along(ds, dz)[1] + c) for ds, dz in offsets] + [sibling])
+    order = list(range(1, seqs)) + [0]
+    gathers = {}
+    for k in order:
+        for ds in range(1, seqs):
+            rows = pl.ds(pl.multiple_of(lax.rem(s + ds + k, seqs) * span, span), span)
+            gathers[k, ds] = remote(
+                g_ref.at[rows],
+                held.at[ds, rows],
+                g_send.at[k, ds],
+                g_recv.at[k, ds],
+                (along(ds, 0)[0], 2 * z + c),
+            )
+            gathers[k, ds].start()
+    pairs, sends = {}, []
+
+    def finish(k):
+        q = lax.rem(s + k, seqs)
+        pairs[k].wait_recv()
+        for dz in range(chips):
+            there = along(0, dz)[1]
+            both = part[q, there, c].astype(jnp.float32) + sib[q, there].astype(jnp.float32)
+            if k == 0 and dz == 0:
+                got[0, 0] = both.astype(jnp.bfloat16)
+            else:
+                pair[k, dz] = both.astype(jnp.bfloat16)
+                sends.append(
+                    remote(
+                        pair.at[k, dz],
+                        got.at[k, dz],
+                        o_send.at[k, dz],
+                        o_recv.at[k, dz],
+                        (q, 2 * there + c),
+                    )
+                )
+                sends[-1].start()
+
+    for step, k in enumerate(order):
+        q = lax.rem(s + k, seqs)
+        rows = pl.ds(pl.multiple_of(q * span, span), span)
+        for ds in range(1, seqs):
+            gathers[k, ds].wait_recv()
+        blocks = [g_ref[rows, :].astype(jnp.float32)] + [
+            held[ds, rows, :].astype(jnp.float32) for ds in range(1, seqs)
+        ]
+        squares = blocks[0] * blocks[0]
+        for b in blocks[1:]:
+            squares = squares + b * b
+        scale = lax.rsqrt(jnp.sum(squares, axis=1, keepdims=True) / (width * seqs) + 1e-05)
+        froms = [pl.multiple_of(lax.rem(s + seqs - ds, seqs) * width, width) for ds in range(seqs)]
+        for ds in range(seqs):
+            normed[ds] = (blocks[ds] * scale * gain_ref[:, pl.ds(froms[ds], width)]).astype(
+                jnp.bfloat16
+            )
+        tile = 256
+
+        def column(n, _):
+            here = pl.ds(pl.multiple_of(n * tile, tile), tile)
+            acc = jnp.zeros((span, tile), jnp.float32)
+            for ds in range(seqs):
+                acc = acc + jnp.dot(
+                    normed[ds],
+                    w_ref[pl.ds(froms[ds], width), here],
+                    preferred_element_type=jnp.float32,
+                )
+            part[q, :, :, :, here] = acc.astype(jnp.bfloat16).reshape(chips, 2, own, tile)
+            return 0
+
+        lax.fori_loop(0, cols // tile, column, 0)
+        pairs[k] = remote(
+            part.at[q, :, 1 - c], sib.at[q], p_send.at[k], p_recv.at[k], sibling
+        )
+        pairs[k].start()
+        if step:
+            finish(order[step - 1])
+    finish(order[-1])
+    for copy in sends:
+        copy.wait_recv()
+    for ds in range(seqs):
+        total = got[ds, 0].astype(jnp.float32)
+        for dz in range(1, chips):
+            total = total + got[ds, dz].astype(jnp.float32)
+        begin = pl.multiple_of(lax.rem(s + seqs - ds, seqs) * cols, cols)
+        out_ref[:, pl.ds(begin, cols)] = total.astype(jnp.bfloat16)
+    for copy in list(gathers.values()) + list(pairs.values()) + sends:
+        copy.wait_send()
+
+
+def project_out(gated, gain, w_out, own, seqs, chips):
+    total, width = gated.shape
+    cols = w_out.shape[1]
+    dma = pltpu.SemaphoreType.DMA
+    vmem = pl.BlockSpec(memory_space=pltpu.VMEM)
+    return pl.pallas_call(
+        out_kernel,
+        out_shape=jax.ShapeDtypeStruct((own, cols * seqs), jnp.bfloat16),
+        in_specs=[vmem] * 3,
+        out_specs=vmem,
+        scratch_shapes=[
+            pltpu.VMEM((seqs, total, width), jnp.bfloat16),
+            pltpu.VMEM((seqs, total // seqs, width), jnp.bfloat16),
+            pltpu.VMEM((seqs, chips, 2, own, cols), jnp.bfloat16),
+            pltpu.VMEM((seqs, chips, own, cols), jnp.bfloat16),
+            pltpu.VMEM((seqs, chips, own, cols), jnp.bfloat16),
+            pltpu.VMEM((seqs, chips, own, cols), jnp.bfloat16),
+            dma((seqs, seqs)),
+            dma((seqs, seqs)),
+            dma((seqs,)),
+            dma((seqs,)),
+            dma((seqs, chips)),
+            dma((seqs, chips)),
+        ],
+        compiler_params=pltpu.CompilerParams(
+            collective_id=1, has_side_effects=True, vmem_limit_bytes=40 * 2**20
+        ),
+    )(gated, gain[None, :], w_out)
+
+
+def in_kernel(
+    tok_ref, wg_ref, wx_ref, ws_ref, gate_ref, xin_ref, small_ref,
+    tok, mine, mine_s, sent, sent_s, got, got_s,
+    t_send, t_recv, f_send, f_recv, p_send, p_recv, q_send, q_recv,
+):
+    s, z, c, seqs, chips, along = places()
+    own = tok_ref.shape[0]
+    depth = wg_ref.shape[0]
+    width = wg_ref.shape[1] // seqs
+    span = own * chips * 2
+    sibling = (s, 2 * z + 1 - c)
+    offsets = [(ds, dz) for ds in range(seqs) for dz in range(chips) if ds or dz]
+    enter([(along(ds, dz)[0], 2 * along(ds, dz)[1] + c) for ds, dz in offsets] + [sibling])
+    spread = {}
+    for ds, dz in offsets:
+        to, there = along(ds, dz)
+        spread[ds, dz] = remote(
+            tok_ref.at[:, pl.ds(pl.multiple_of(to * depth, depth), depth)],
+            tok.at[ds, z, c],
+            t_send.at[ds, dz],
+            t_recv.at[ds, dz],
+            (to, 2 * there + c),
+        )
+        spread[ds, dz].start()
+    tok[0, z, c] = tok_ref[:, pl.ds(pl.multiple_of(s * depth, depth), depth)]
+    forwards, sums = [], []
+
+    def forward(k):
+        for ds, dz in offsets:
+            if ds == k:
+                spread[ds, dz].wait_recv()
+        forwards.append(
+            remote(tok.at[k, :, c], tok.at[k, :, c], f_send.at[k], f_recv.at[k], sibling)
+        )
+        forwards[k].start()
+
+    forward(0)
+    for k in range(seqs):
+        forwards[k].wait_recv()
+        if k + 1 < seqs:
+            forward(k + 1)
+        q = lax.rem(s + seqs - k, seqs)
+        for ds in list(range(1, seqs)) + [0]:
+            to = along(ds, 0)[0]
+            cols = pl.ds(pl.multiple_of(to * width, width), width)
+            rows = tok[k].reshape(span, depth)
+            gate = jnp.dot(rows, wg_ref[:, cols], preferred_element_type=jnp.float32)
+            xin = jnp.dot(rows, wx_ref[:, cols], preferred_element_type=jnp.float32)
+            small = lax.dot_general(
+                ws_ref[to], rows, (((1,), (1,)), ((), ())), preferred_element_type=jnp.float32
+            )
+            if ds == 0:
+                mine[q, :, :width] = gate
+                mine[q, :, width:] = xin
+                mine_s[q] = small
+                continue
+            sent[ds, k, :, :width] = gate.astype(jnp.bfloat16)
+            sent[ds, k, :, width:] = xin.astype(jnp.bfloat16)
+            sent_s[ds, k] = small.astype(jnp.bfloat16)
+            peer = (to, 2 * z + c)
+            for copy in (
+                remote(sent.at[ds, k], got.at[ds, q], p_send.at[ds, k], p_recv.at[ds, k], peer),
+                remote(
+                    sent_s.at[ds, k], got_s.at[ds, q], q_send.at[ds, k], q_recv.at[ds, k], peer
+                ),
+            ):
+                copy.start()
+                sums.append(copy)
+    for copy in sums:
+        copy.wait_recv()
+
+    def add(q, _):
+        rows = pl.ds(pl.multiple_of(q * span, span), span)
+        total, small = mine[q], mine_s[q]
+        for ds in range(1, seqs):
+            total = total + got[ds, q].astype(jnp.float32)
+            small = small + got_s[ds, q].astype(jnp.float32)
+        gate_ref[rows, :] = total[:, :width].astype(jnp.bfloat16)
+        xin_ref[rows, :] = total[:, width:].astype(jnp.bfloat16)
+        small_ref[:, rows] = small.astype(jnp.bfloat16)
+        return 0
+
+    lax.fori_loop(0, seqs, add, 0)
+    for copy in list(spread.values()) + forwards + sums:
+        copy.wait_send()
+
+
+def project_in(tokens, w_gate, w_xin, w_small, seqs, chips):
+    own = tokens.shape[0]
+    depth = w_gate.shape[0]
+    width = w_gate.shape[1] // seqs
+    span = own * chips * 2
+    few = w_small.shape[1]
+    dma = pltpu.SemaphoreType.DMA
+    vmem = pl.BlockSpec(memory_space=pltpu.VMEM)
+    return pl.pallas_call(
+        in_kernel,
+        out_shape=(
+            jax.ShapeDtypeStruct((span * seqs, width), jnp.bfloat16),
+            jax.ShapeDtypeStruct((span * seqs, width), jnp.bfloat16),
+            jax.ShapeDtypeStruct((few, span * seqs), jnp.bfloat16),
+        ),
+        in_specs=[vmem] * 4,
+        out_specs=(vmem,) * 3,
+        scratch_shapes=[
+            pltpu.VMEM((seqs, chips, 2, own, depth), jnp.bfloat16),
+            pltpu.VMEM((seqs, span, 2 * width), jnp.float32),
+            pltpu.VMEM((seqs, few, span), jnp.float32),
+            pltpu.VMEM((seqs, seqs, span, 2 * width), jnp.bfloat16),
+            pltpu.VMEM((seqs, seqs, few, span), jnp.bfloat16),
+            pltpu.VMEM((seqs, seqs, span, 2 * width), jnp.bfloat16),
+            pltpu.VMEM((seqs, seqs, few, span), jnp.bfloat16),
+            dma((seqs, chips)),
+            dma((seqs, chips)),
+            dma((seqs,)),
+            dma((seqs,)),
+            dma((seqs, seqs)),
+            dma((seqs, seqs)),
+            dma((seqs, seqs)),
+            dma((seqs, seqs)),
+        ],
+        compiler_params=pltpu.CompilerParams(
+            collective_id=2, has_side_effects=True, vmem_limit_bytes=48 * 2**20
+        ),
+    )(tokens, w_gate, w_xin, w_small)
+
+
 def conv_full(values, weights, bias, docs, axis):
     count = values.shape[axis]
     values = values.astype(jnp.float32)
@@ -282,26 +569,17 @@
     chans = w_gate.shape[1] // seqs
     heads = w_dt.shape[1] // seqs
     parts = w_bc.shape[1] // (seqs * GROUPS)
-    columns = lax.all_to_all(tokens, "seq", 1, 0, tiled=True)
-    rows = lax.all_gather(columns, "tensor", axis=0)
-    rows = rows.reshape(tens, seqs, own, depth).transpose(1, 0, 2, 3).reshape(total, depth)
-
-    def project(weight):
-        return jnp.dot(rows, weight, preferred_element_type=jnp.float32).astype(jnp.bfloat16)
-
-    gate = lax.psum_scatter(project(w_gate), "seq", scatter_dimension=1, tiled=True)
-    xin = lax.psum_scatter(project(w_xin), "seq", scatter_dimension=1, tiled=True)
     small = jnp.concatenate(
         [
             w_bc.T.reshape(seqs, parts, GROUPS, depth)
             .transpose(0, 2, 1, 3)
             .reshape(seqs, parts * GROUPS, depth),
             w_dt.T.reshape(seqs, heads, depth),
+            jnp.zeros((seqs, -(parts * GROUPS + heads) % 16, depth), jnp.bfloat16),
         ],
         axis=1,
     )
-    small = jnp.einsum("scd,td->sct", small, rows, preferred_element_type=jnp.float32)
-    small = lax.psum_scatter(small.astype(jnp.bfloat16), "seq", scatter_dimension=0, tiled=True)[0]
+    gate, xin, small = project_in(tokens, w_gate, w_xin, small, seqs, tens // 2)
     docs = doc_ids(lengths, jnp.arange(total, dtype=jnp.int32))
 
     def mine(vector, width, axis=0):
@@ -317,20 +595,14 @@
     bcc = conv_full(small[: parts * GROUPS], grouped(conv_bc), grouped(conv_bc_bias), docs, 1)
     bcc = lax.all_to_all(bcc.reshape(GROUPS, parts, total), "tensor", 0, 0, tiled=True)
     bcc = lax.all_gather(bcc, "seq", axis=0).transpose(1, 0, 2, 3).reshape(2 * STATE, total)
-    dtin = small[parts * GROUPS :].T.astype(jnp.float32)
+    dtin = small[parts * GROUPS : parts * GROUPS + heads].T.astype(jnp.float32)
     dtv = jax.nn.softplus(dtin + mine(dt_bias, heads)[None, :])
     y = scan_heads(
         xc, dtv, mine(decay_rate, heads), bcc[:STATE], bcc[STATE:], docs, min(STRETCH, total)
     )
     y = y + jnp.repeat(mine(d_skip, heads), HDIM)[None, :] * xc.astype(jnp.float32)
     gated = (y * jax.nn.silu(gate.astype(jnp.float32))).astype(jnp.bfloat16)
-    gated = lax.all_gather(gated, "seq", axis=1, tiled=True).astype(jnp.float32)
-    mean = jnp.mean(gated * gated, axis=1, keepdims=True)
-    normed = (gated * lax.rsqrt(mean + 1e-05) * norm_gain[None, :]).astype(jnp.bfloat16)
-    out = jnp.dot(normed, w_out, preferred_element_type=jnp.float32).astype(jnp.bfloat16)
-    out = out.reshape(seqs, tens, own, depth).transpose(1, 0, 2, 3)
-    out = lax.psum_scatter(out, "tensor", scatter_dimension=0, tiled=True)[0]
-    return lax.all_to_all(out, "seq", 0, 2, tiled=True)[0]
+    return project_out(gated, norm_gain, w_out, own, seqs, tens // 2)
 
 
 def solution(mesh):

time: 305 us -> 180 us (0.59)
  waiting for transfers between devices: 184 us -> 0.01 us
  Pallas kernels: 0 us -> 132 us
  blocking collectives: 32.2 us -> 10.8 us
  matrix products: 22.9 us -> 3.91 us
  between operations: 13.8 us -> 0.36 us
  local copies, waits for them, and re-layouts: 26.5 us -> 14.8 us
  other arithmetic: 19.3 us -> 13.7 us
    pallas_call x0 -> x2, Pallas kernels: none -> 132 us  [the longest x1 82.2 us: project_in(): pl.pallas_call(in_kernel, out_shape=(jax.ShapeDtypeStruct((span * seqs, w...]
    unnamed x8 -> x0, waiting for transfers between devices: 92.6 us -> none
    all_gather x2 -> x0, waiting for transfers between devices: 61.9 us -> none  [the longest x1 35.3 us: shards(): gated = lax.all_gather(gated, 'seq', axis=1, tiled=True).astype(jnp.float32)]
    reduce_scatter x2 -> x0, waiting for transfers between devices: 23.5 us -> none  [the longest x1 20.2 us: shards(): lax.psum_scatter(project(w_gate), 'seq', scatter_dimension=1, tiled=True)]
    all_to_all x2 -> x0, blocking collectives: 20 us -> none  [the longest x1 10.8 us: shards(): columns = lax.all_to_all(tokens, 'seq', 1, 0, tiled=True)]
    dot_general x4 -> x0, matrix products: 18.1 us -> none  [the longest x2 11.1 us: project(): jnp.dot(rows, weight, preferred_element_type=jnp.float32)]
    all_to_all x1, waiting for transfers between devices: 6.26 us -> 0.01 us  [shards(): lax.all_to_all(bcc.reshape(GROUPS, parts, total), 'tensor', 0, 0, tiled=T...]
  transfers between devices with their start and end apart: 7 -> 1, of which waited for: 7 -> 0; matrix products, arithmetic and copies ran while one was open for 16% -> 8% of each run, Pallas kernels for 0% -> 0%
where the time goes in v2:
time: 180 us
  Pallas kernels  132 us (73%)
  local copies, waits for them, and re-layouts  14.8 us (8%)
  other arithmetic  13.7 us (8%)
  blocking collectives  10.8 us (6%)
  starting transfers between devices  4.32 us (2%)
  matrix products  3.91 us (2%)
    pallas_call x1, Pallas kernels, project_in(): pl.pallas_call(in_kernel, out_shape=(jax.ShapeDtypeStruct((span * seqs, w...  82.2 us
    pallas_call x1, Pallas kernels, project_out(): pl.pallas_call(out_kernel, out_shape=jax.ShapeDtypeStruct((own, cols * se...  49.9 us
    all_gather x1, blocking collectives, shards(): lax.all_gather(bcc, 'seq', axis=0).transpose(1, 0, 2, 3)  10.8 us
    another operation x5, other arithmetic  6.02 us
    all_to_all x1, starting transfers between devices, shards(): lax.all_to_all(bcc.reshape(GROUPS, parts, total), 'tensor', 0, 0, tiled=T...  4.32 us
    reshape x2, local copies, waits for them, and re-layouts, scan_heads(): return (inner + outer * carry_in[..., None]).reshape(count, heads * HDIM)  3.99 us
  transfers between devices with their start and end apart: 1, of which 0 were waited for; matrix products, arithmetic and copies ran while one was open for 8% of the time, Pallas kernels for 0%

profile of v2, /device:TPU:0, one launch (start us, length us, event | category | flops | bytes accessed | tf_op | source)
XLA Modules:
  0.0 179.9 jit_solution(8239982424944370787)
XLA Ops:
  0.0 1.0 reduce-window.19
  1.0 0.7 bitcast_subtract_fusion
  2.0 1.2 copy.157
  3.2 0.3 copy.203
  5.0 0.9 copy-done.3
  6.0 82.2 %shard_map.145 = (bf16[1024,256]{1,0:T(8,128)(2,1)S(1)}, bf16[1024,256]{1,0:T(8,128)(2,1)S(1)}, bf16[80,1024]{1,0:T(8,128)(2,1)S(1)}) custom-call(bf16[32,4096]{1,0:T(8,128)(2,1)S(1)} %copy-done.3, bf16[1024,1024]{1,0:T(8,128)(2,1)S(1)} %copy-done.1, bf16[1024,1024]{1,0:T(8,128)(2,1)} %wx_ref.1, bf16[4,80,1024]{2,1,0:T(8,128)(2,1)S(1)} %maximum_maximum_fusion.ws_ref), custom_call_target="tpu_custom_call" | custom-call | tf_op jit(solution)/shard_map/pallas_call | solution.py:460
  88.3 1.0 fusion.30
  89.3 4.3 %all-to-all-start = ((bf16[8,8,1024]{2,1,0:T(8,128)(2,1)}), bf16[8,8,1024]{2,1,0:T(8,128)(2,1)S(1)}, u32[]{:S(2)}, u32[]{:S(2)}) async-start(bf16[8,8,1024]{2,1,0:T(8,128)(2,1)} %fusion.30), calls=%async_computation | async-start | bytes 262144 | tf_op jit(solution)/shard_map/all_to_all | solution.py:596
  94.1 1.1 slice.161
  95.2 1.1 slice.162
  96.7 4.8 %reduce-window.20 = f32[4,4,2,128]{3,2,1,0:T(2,128)S(1)} reduce-window(f32[4,4,2,128]{3,2,1,0:T(2,128)S(1)} %copy.183, f32[]{:T(128)} %constant.24.clone.1), window={size=1x1x1x128 pad=0_0x0_0x0_0x127_0}, to_apply=%region_2.3 | reduce-window | flops 520192 | bytes 32772 | tf_op jit(solution)/shard_map/reduce-window.1
  102.4 0.8 dynamic_slice.22
  103.2 0.9 fusion.43
  104.1 2.5 %multiply_convert_fusion.5 = bf16[1024,256]{1,0:T(8,128)(2,1)S(1)} fusion(f32[1021,256]{1,0:T(8,128)} %slice.162, f32[1022,256]{1,0:T(8,128)} %slice.161, f32[1023,256]{1,0:T(8,128)S(1)} %slice.160, f32[1024]{0:T(1024)S(1)} %get-tuple-element.32, f32[256]{0:T(256)S(1)} %bitcast.86, f32[1024]{0:T(1024)S(1)} %pad_convert_fusion.1, f32[256]{0:T(256)S(1)} %bitcast.84, ...), kind=kLoop, calls=%fused_computation.18 | loop fusion | flops 4456448 | bytes 4205568 | tf_op jit(solution)/shard_map/convert_element_type | solution.py:511
  106.8 0.4 reshape.199
  108.2 10.8 %all-gather = bf16[32,8,1024]{2,1,0:T(8,128)(2,1)S(1)} all-gather(bf16[8,8,1024]{2,1,0:T(8,128)(2,1)S(1)} %all-to-all-done), channel_id=2, replica_groups=mesh['seq'=4,'tensor'=8] {'seq'}, dimensions={0}, use_global_device_ids=true | all-gather | bytes 655360 | tf_op jit(solution)/shard_map/all_gather | solution.py:597
  119.4 0.3 fusion.25
  120.1 1.9 %fusion.7 = f32[4,256,4,64]{1,3,2,0:T(8,128)S(1)} fusion(f32[4,4,256]{2,1,0:T(4,128)S(1)} %copy.172, f32[4,4,256]{2,1,0:T(4,128)S(1)} %reduce_window_sum.31, f32[4,256,256]{2,1,0:T(8,128)S(1)} %fusion.25, pred[4,256,256]{2,1,0:T(8,128)(4,1)S(1)} %compare_and_fusion, bf16[4,256,4,64]{1,0,3,2:T(4,128)(2,1)S(1)} %reshape.199), kind=kOutput, calls=%fused_computation.8 | convolution fusion | flops 139460608 | bytes 2916352 | tf_op jit(solution)/shard_map/bhij,bjhp->bihp/dot_general | solution.py:530
  122.1 1.3 fusion.8
  123.5 1.8 %copy.188 = f32[4,256,4,64]{3,2,1,0:T(4,128)S(1)} copy(f32[4,256,4,64]{1,3,2,0:T(8,128)} %fusion.8) | data formatting | bytes 2097152 | tf_op jit(solution)/shard_map/reshape | solution.py:544
  125.3 2.2 %reshape.213 = f32[1024,256]{1,0:T(8,128)} reshape(f32[4,256,4,64]{3,2,1,0:T(4,128)S(1)} %copy.188) | data formatting | bytes 2097152 | tf_op jit(solution)/shard_map/reshape | solution.py:544
  127.5 1.8 fusion.13.g_ref
  129.4 49.9 %shard_map.146 = bf16[32,4096]{1,0:T(8,128)(2,1)S(1)} custom-call(bf16[1024,256]{1,0:T(8,128)(2,1)S(1)} %fusion.13.g_ref, f32[1,1024]{1,0:T(1,128)S(1)} %bitcast.68, bf16[1024,1024]{1,0:T(8,128)(2,1)S(1)} %copy-done.2), custom_call_target="tpu_custom_call" | custom-call | tf_op jit(solution)/shard_map/pallas_call | solution.py:340
  179.2 0.7 copy.205
  (87 shorter events, 5.7 us)
Async XLA Ops:
  0.0 3.6 %copy-start = (f32[4,256]{1,0:T(4,128)S(1)}, f32[4,256]{1,0:T(4,128)}, u32[]{:S(2)}) copy-start(f32[4,256]{1,0:T(4,128)} %param.22) | copy-start | bytes 12292
  0.0 3.5 %copy-start.5 = (bf16[1024,16]{0,1:T(8,128)(2,1)S(1)}, bf16[1024,16]{0,1:T(8,128)(2,1)}, u32[]{:S(2)}) copy-start(bf16[1024,16]{0,1:T(8,128)(2,1)} %param.19) | copy-start | bytes 98308
  0.0 4.4 %copy-start.6 = (f32[256]{0:T(256)S(1)}, f32[256]{0:T(256)}, u32[]{:S(2)}) copy-start(f32[256]{0:T(256)} %param.23) | copy-start | bytes 3076
  0.0 5.0 %copy-start.1 = (bf16[1024,1024]{1,0:T(8,128)(2,1)S(1)}, bf16[1024,1024]{1,0:T(8,128)(2,1)}, u32[]{:S(2)}) copy-start(bf16[1024,1024]{1,0:T(8,128)(2,1)} %wg_ref.1) | copy-start | bytes 6291460
  5.0 1.0 copy-start.3
  89.3 18.9 %all-to-all-start = ((bf16[8,8,1024]{2,1,0:T(8,128)(2,1)}), bf16[8,8,1024]{2,1,0:T(8,128)(2,1)S(1)}, u32[]{:S(2)}, u32[]{:S(2)}) async-start(bf16[8,8,1024]{2,1,0:T(8,128)(2,1)} %fusion.30), calls=%async_computation | async-start | bytes 262144 | tf_op jit(solution)/shard_map/all_to_all | solution.py:596
  94.1 2.2 %copy-start.7 = (f32[16]{0:T(128)S(1)}, f32[16]{0:T(128)}, u32[]{:S(2)}) copy-start(f32[16]{0:T(128)} %param.24) | copy-start | bytes 196
  94.1 2.4 %copy-start.8 = (f32[16]{0:T(128)S(1)}, f32[16]{0:T(128)}, u32[]{:S(2)}) copy-start(f32[16]{0:T(128)} %param.25) | copy-start | bytes 196
  106.6 0.8 copy-start.9
  127.5 1.9 %copy-start.2 = (bf16[1024,1024]{1,0:T(8,128)(2,1)S(1)}, bf16[1024,1024]{1,0:T(8,128)(2,1)}, u32[]{:S(2)}) copy-start(bf16[1024,1024]{1,0:T(8,128)(2,1)} %w_ref.1) | copy-start | bytes 6291460
  127.5 1.9 %copy-start.4 = (f32[1024]{0:T(1024)S(1)}, f32[1024]{0:T(1024)}, u32[]{:S(2)}) copy-start(f32[1024]{0:T(1024)} %param.27) | copy-start | bytes 12292

commit v3 on v2

--- a/solution.py
+++ b/solution.py
@@ -489,6 +489,56 @@
     )(tokens, w_gate, w_xin, w_small)
 
 
+def group_kernel(in_ref, out_ref, held, t_send, t_recv, s_send, s_recv):
+    s, t = lax.axis_index("seq"), lax.axis_index("tensor")
+    seqs, tens = lax.axis_size("seq"), lax.axis_size("tensor")
+    across = [(s, lax.rem(t + dt, tens)) for dt in range(1, tens)]
+    along = [(lax.rem(s + ds, seqs), t) for ds in range(1, seqs)]
+    enter(across + along)
+    first = [
+        remote(in_ref.at[peer[1]], held.at[0, t], t_send.at[dt], t_recv.at[dt], peer)
+        for dt, peer in enumerate(across)
+    ]
+    for copy in first:
+        copy.start()
+    held[0, t] = in_ref[t]
+    for copy in first:
+        copy.wait_recv()
+    second = [
+        remote(held.at[0], held.at[1 + ds], s_send.at[ds], s_recv.at[ds], peer)
+        for ds, peer in enumerate(along)
+    ]
+    for copy in second:
+        copy.start()
+    for copy in second:
+        copy.wait_recv()
+    out_ref[...] = held[...]
+    for copy in first + second:
+        copy.wait_send()
+
+
+def to_groups(values, seqs):
+    tens, rows, cols = values.shape
+    dma = pltpu.SemaphoreType.DMA
+    vmem = pl.BlockSpec(memory_space=pltpu.VMEM)
+    return pl.pallas_call(
+        group_kernel,
+        out_shape=jax.ShapeDtypeStruct((seqs, tens, rows, cols), values.dtype),
+        in_specs=[vmem],
+        out_specs=vmem,
+        scratch_shapes=[
+            pltpu.VMEM((seqs, tens, rows, cols), values.dtype),
+            dma((tens - 1,)),
+            dma((tens - 1,)),
+            dma((seqs - 1,)),
+            dma((seqs - 1,)),
+        ],
+        compiler_params=pltpu.CompilerParams(
+            collective_id=3, has_side_effects=True, vmem_limit_bytes=16 * 2**20
+        ),
+    )(values)
+
+
 def conv_full(values, weights, bias, docs, axis):
     count = values.shape[axis]
     values = values.astype(jnp.float32)
@@ -516,7 +566,8 @@
     blocks = count // block
     xh = xc.reshape(blocks, block, heads, HDIM)
     dtb = dtv.reshape(blocks, block, heads)
-    cum = jnp.cumsum(-dtb * rate[None, None, :], axis=1)
+    upto = jnp.tril(jnp.ones((block, block), jnp.float32))
+    cum = jnp.einsum("ij,bjh->bih", upto, -dtb * rate[None, None, :], precision=HIGH)
     docb = docs.reshape(blocks, block)
     bb = bmat.reshape(STATE, blocks, block)
     cb = cmat.reshape(STATE, blocks, block)
@@ -593,8 +644,11 @@
         return jnp.swapaxes(vector, -1, -2).reshape(lead + (parts * GROUPS,))
 
     bcc = conv_full(small[: parts * GROUPS], grouped(conv_bc), grouped(conv_bc_bias), docs, 1)
-    bcc = lax.all_to_all(bcc.reshape(GROUPS, parts, total), "tensor", 0, 0, tiled=True)
-    bcc = lax.all_gather(bcc, "seq", axis=0).transpose(1, 0, 2, 3).reshape(2 * STATE, total)
+    fold = 16 // parts
+    bcc = bcc.reshape(GROUPS, parts, fold, total // fold).transpose(0, 2, 1, 3)
+    bcc = to_groups(bcc.reshape(GROUPS, 16, total // fold), seqs)
+    bcc = bcc.reshape(seqs, tens, fold, parts, total // fold).transpose(1, 0, 3, 2, 4)
+    bcc = bcc.reshape(2 * STATE, total)
     dtin = small[parts * GROUPS : parts * GROUPS + heads].T.astype(jnp.float32)
     dtv = jax.nn.softplus(dtin + mine(dt_bias, heads)[None, :])
     y = scan_heads(
@@ -608,7 +662,7 @@
 def solution(mesh):
     seqs, tens = mesh.shape["seq"], mesh.shape["tensor"]
     heads = INNER // HDIM
-    narrow = tens == GROUPS and heads % (seqs * tens) == 0 and 2 * STATE % (seqs * tens) == 0
+    narrow = tens == GROUPS and heads % (seqs * tens) == 0 and 2 * STATE == 8 * seqs * tens
     body = shards if narrow else shards_wide
     in_specs = (
         P(("seq", "tensor"), None),

time: 180 us -> 173 us (0.961); the launches traced: 180 us -> 171 us
  Pallas kernels: 132 us -> 145 us
  blocking collectives: 10.8 us -> 0 us
  other arithmetic: 13.7 us -> 6 us
  starting transfers between devices: 4.32 us -> 0 us
    pallas_call x0 -> x1, Pallas kernels: none -> 15.7 us  [to_groups(): pl.pallas_call(group_kernel, out_shape=jax.ShapeDtypeStruct((seqs, tens,...]
    all_gather x1 -> x0, blocking collectives: 10.8 us -> none  [shards(): lax.all_gather(bcc, 'seq', axis=0).transpose(1, 0, 2, 3)]
    another operation x5 -> x2, other arithmetic: 6.02 us -> 0.9 us
    all_to_all x1 -> x0, starting transfers between devices: 4.32 us -> none  [shards(): lax.all_to_all(bcc.reshape(GROUPS, parts, total), 'tensor', 0, 0, tiled=T...]
    pallas_call x1, Pallas kernels: 49.9 us -> 47.1 us  [project_out(): pl.pallas_call(out_kernel, out_shape=jax.ShapeDtypeStruct((own, cols * se...]
    slice x3, local copies, waits for them, and re-layouts: 2.25 us -> 0.22 us  [conv_full(): kept = lax.slice_in_dim(values, 0, count - back, axis=axis)]
  transfers between devices with their start and end apart: 1 -> 0, of which waited for: 0 -> 0; matrix products, arithmetic and copies ran while one was open for 8% -> 0% of each run, Pallas kernels for 0% -> 0%
where the time goes in v3:
time: 173 us; the launch traced here: 171 us
  Pallas kernels  145 us (84%)
  local copies, waits for them, and re-layouts  14.5 us (8%)
  other arithmetic  6 us (3%)
  matrix products  5.24 us (3%)
    pallas_call x1, Pallas kernels, project_in(): pl.pallas_call(in_kernel, out_shape=(jax.ShapeDtypeStruct((span * seqs, w...  82.2 us
    pallas_call x1, Pallas kernels, project_out(): pl.pallas_call(out_kernel, out_shape=jax.ShapeDtypeStruct((own, cols * se...  47.1 us
    pallas_call x1, Pallas kernels, to_groups(): pl.pallas_call(group_kernel, out_shape=jax.ShapeDtypeStruct((seqs, tens,...  15.7 us
    reshape x2, local copies, waits for them, and re-layouts, scan_heads(): return (inner + outer * carry_in[..., None]).reshape(count, heads * HDIM)  3.98 us

profile of v3, /device:TPU:0, one launch (start us, length us, event | category | flops | bytes accessed | tf_op | source)
XLA Modules:
  0.0 171.1 jit_solution(12478515096696369604)
XLA Ops:
  0.0 0.9 dynamic_slice.25
  0.9 1.2 copy.68
  2.1 0.3 copy.112
  2.8 0.9 copy-done.3
  3.7 82.2 %shard_map.145 = (bf16[1024,256]{1,0:T(8,128)(2,1)S(1)}, bf16[1024,256]{1,0:T(8,128)(2,1)S(1)}, bf16[80,1024]{1,0:T(8,128)(2,1)S(1)}) custom-call(bf16[32,4096]{1,0:T(8,128)(2,1)S(1)} %copy-done.3, bf16[1024,1024]{1,0:T(8,128)(2,1)S(1)} %copy-done.1, bf16[1024,1024]{1,0:T(8,128)(2,1)} %wx_ref.1, bf16[4,80,1024]{2,1,0:T(8,128)(2,1)S(1)} %maximum_maximum_fusion.ws_ref), custom_call_target="tpu_custom_call" | custom-call | tf_op jit(solution)/shard_map/pallas_call | solution.py:460
  86.1 0.3 fusion.25
  87.6 0.9 fusion.50
  88.5 0.8 dynamic_slice.22
  89.9 1.3 multiply_convert_fusion.5
  91.5 0.4 reshape.176
  93.2 0.3 multiply_convert_fusion.6
  93.5 15.7 %shard_map.146 = bf16[4,8,16,512]{3,2,1,0:T(8,128)(2,1)S(1)} custom-call(bf16[8,16,512]{2,1,0:T(8,128)(2,1)S(1)} %bitcast.66), custom_call_target="tpu_custom_call" | custom-call | tf_op jit(solution)/shard_map/pallas_call | solution.py:524
  109.2 0.5 copy.111
  109.7 0.4 fusion.49
  110.7 0.7 fusion.48
  111.6 0.3 fusion.27
  111.9 0.7 reshape.184
  113.0 2.9 %fusion.7 = f32[4,256,4,64]{1,3,2,0:T(8,128)S(1)} fusion(f32[4,4,256]{2,1,0:T(4,128)S(1)} %copy.80, f32[4,4,256]{2,1,0:T(4,128)} %copy-done.9, f32[4,256,256]{2,1,0:T(8,128)S(1)} %fusion.27, pred[4,256,256]{2,1,0:T(8,128)(4,1)S(1)} %compare_and_fusion, bf16[4,256,4,64]{1,0,3,2:T(4,128)(2,1)S(1)} %reshape.176), kind=kOutput, calls=%fused_computation.8 | convolution fusion | flops 139460608 | bytes 2916352 | tf_op jit(solution)/shard_map/bhij,bjhp->bihp/dot_general | solution.py:581
  115.9 1.3 fusion.8
  117.3 1.8 %copy.95 = f32[4,256,4,64]{3,2,1,0:T(4,128)S(1)} copy(f32[4,256,4,64]{1,3,2,0:T(8,128)} %fusion.8) | data formatting | bytes 2097152 | tf_op jit(solution)/shard_map/reshape | solution.py:595
  119.1 2.1 %reshape.189 = f32[1024,256]{1,0:T(8,128)} reshape(f32[4,256,4,64]{3,2,1,0:T(4,128)S(1)} %copy.95) | data formatting | bytes 2097152 | tf_op jit(solution)/shard_map/reshape | solution.py:595
  121.5 1.7 %fusion.13.g_ref = bf16[1024,256]{1,0:T(8,128)(2,1)S(1)} fusion(bf16[1024,256]{1,0:T(8,128)(2,1)S(1)} %get-tuple-element.10, f32[1024,256]{1,0:T(8,128)} %reshape.189, bf16[1024,256]{1,0:T(8,128)(2,1)S(1)} %multiply_convert_fusion.5, f32[256]{0:T(256)S(1)} %mul.324), kind=kLoop, calls=%fused_computation.19 | loop fusion | flops 2621440 | bytes 2622464 | tf_op jit(solution)/shard_map/convert_element_type | solution.py:658
  123.3 47.1 %shard_map.147 = bf16[32,4096]{1,0:T(8,128)(2,1)S(1)} custom-call(bf16[1024,256]{1,0:T(8,128)(2,1)S(1)} %fusion.13.g_ref, f32[1,1024]{1,0:T(1,128)S(1)} %bitcast.67, bf16[1024,1024]{1,0:T(8,128)(2,1)S(1)} %copy-done.2), custom_call_target="tpu_custom_call" | custom-call | tf_op jit(solution)/shard_map/pallas_call | solution.py:340
  170.4 0.7 copy.114
  (84 shorter events, 4.9 us)
Async XLA Ops:
  0.0 92.1 %copy-start = (f32[4,256]{1,0:T(4,128)S(1)}, f32[4,256]{1,0:T(4,128)}, u32[]{:S(2)}) copy-start(f32[4,256]{1,0:T(4,128)} %param.22) | copy-start | bytes 12292
  0.0 2.4 %copy-start.10 = (bf16[1024,16]{0,1:T(8,128)(2,1)S(1)}, bf16[1024,16]{0,1:T(8,128)(2,1)}, u32[]{:S(2)}) copy-start(bf16[1024,16]{0,1:T(8,128)(2,1)} %param.19) | copy-start | bytes 98308
  0.0 2.7 %copy-start.1 = (bf16[1024,1024]{1,0:T(8,128)(2,1)S(1)}, bf16[1024,1024]{1,0:T(8,128)(2,1)}, u32[]{:S(2)}) copy-start(bf16[1024,1024]{1,0:T(8,128)(2,1)} %wg_ref.1) | copy-start | bytes 6291460
  2.8 1.0 copy-start.3
  3.7 82.3 %copy-start.12 = (f32[16]{0:T(128)S(1)}, f32[16]{0:T(128)}, u32[]{:S(2)}) copy-start(f32[16]{0:T(128)} %param.25) | copy-start | bytes 196
  3.7 82.9 %copy-start.13 = (s32[8]{0:T(128)S(1)}, s32[8]{0:T(128)}, u32[]{:S(2)}) copy-start(s32[8]{0:T(128)} %param.29) | copy-start | bytes 100
  86.0 3.5 %copy-start.6 = (f32[1024,4]{0,1:T(4,128)}, f32[1024,4]{0,1:T(4,128)S(1)}, u32[]{:S(2)}) copy-start(f32[1024,4]{0,1:T(4,128)S(1)} %compare_select_fusion) | copy-start | bytes 49156
  86.5 3.2 %copy-start.9 = (f32[4,4,256]{2,1,0:T(4,128)}, f32[4,4,256]{2,1,0:T(4,128)S(1)}, u32[]{:S(2)}) copy-start(f32[4,4,256]{2,1,0:T(4,128)S(1)} %fusion.25) | copy-start | bytes 49156
  87.6 22.9 %copy-start.7 = (f32[4,256,4]{1,2,0:T(4,128)}, f32[4,256,4]{1,2,0:T(4,128)S(1)}, u32[]{:S(2)}) copy-start(f32[4,256,4]{1,2,0:T(4,128)S(1)} %get-tuple-element.20) | copy-start | bytes 49156
  91.2 1.6 copy-start.11
  112.9 3.0 %copy-start.5 = (bf16[1,4,64,128]{3,2,1,0:T(8,128)(2,1)S(1)}, bf16[1,4,64,128]{3,2,1,0:T(8,128)(2,1)}, u32[]{:S(2)}) copy-start(bf16[1,4,64,128]{3,2,1,0:T(8,128)(2,1)} %get-tuple-element.16) | copy-start | bytes 196612
  112.9 3.0 %copy-start.8 = (f32[4,256,4]{1,2,0:T(4,128)S(1)}, f32[4,256,4]{1,2,0:T(4,128)}, u32[]{:S(2)}) copy-start(f32[4,256,4]{1,2,0:T(4,128)} %copy-done.7) | copy-start | bytes 49156
  119.1 2.2 %copy-start.14 = (f32[16]{0:T(128)S(1)}, f32[16]{0:T(128)}, u32[]{:S(2)}) copy-start(f32[16]{0:T(128)} %param.26) | copy-start | bytes 196
  121.3 2.0 %copy-start.2 = (bf16[1024,1024]{1,0:T(8,128)(2,1)S(1)}, bf16[1024,1024]{1,0:T(8,128)(2,1)}, u32[]{:S(2)}) copy-start(bf16[1024,1024]{1,0:T(8,128)(2,1)} %w_ref.1) | copy-start | bytes 6291460
  121.3 2.0 %copy-start.4 = (f32[1024]{0:T(1024)S(1)}, f32[1024]{0:T(1024)}, u32[]{:S(2)}) copy-start(f32[1024]{0:T(1024)} %param.27) | copy-start | bytes 12292
